TPU v7x, 512 devices: a whole 4x8x8 slice. The times are simulated.
512 devices in a mesh: prow: 16 (over z, core), pcol: 32 (over y, x).
Axes of the slice: x: 4, y: 8, z: 8, core: 2. Of those that a mesh axis runs over, the one named last changes fastest.
Arguments:
- right_side: float32 [3, 16, 32, 64, 256], P(None, 'prow', 'pcol'), may hold values from -6 to 6
- live_width: int32 [3, 16, 32], P(None, 'prow', 'pcol'), may hold values from 64 to 256
- lower_inverse: bfloat16 [3, 16, 32, 256, 256], P(None, 'prow', 'pcol'), as said below
- upper_inverse: bfloat16 [3, 16, 32, 256, 256], P(None, 'prow', 'pcol'), as said below
- lower_blocks: bfloat16 [3, 16, 32, 4, 256, 256], P(None, 'prow', 'pcol'), may hold values from -0.109375 to 0.109375
- lower_source: int32 [3, 16, 32, 4], P(None, 'prow', 'pcol'), may hold values from 0 to 31
- lower_target: int32 [3, 16, 32, 4], P(None, 'prow', 'pcol'), may hold values from 0 to 15
- upper_blocks: bfloat16 [3, 16, 32, 4, 256, 256], P(None, 'prow', 'pcol'), may hold values from -0.109375 to 0.109375
- upper_source: int32 [3, 16, 32, 4], P(None, 'prow', 'pcol'), may hold values from 0 to 31
- upper_target: int32 [3, 16, 32, 4], P(None, 'prow', 'pcol'), may hold values from 0 to 15
Outputs:
- forward_solution: float32 [3, 16, 32, 64, 256], P(None, 'prow', 'pcol')
- solution: float32 [3, 16, 32, 64, 256], P(None, 'prow', 'pcol')
Inputs may be any that keep to these rules, and one draw needn't show every extreme that they name: lower_inverse[v, a, b] is upper triangular with unit diagonal. upper_inverse[v, a, b] is lower triangular with a positive diagonal.
All inputs are finite; a program needn't handle non-finite values.
Results may differ from a plain program's by a relative error of at most 0.023.
Values may be sent and summed in bfloat16 or wider, within the bound.
A program may use at most 64 MiB of HBM per device.

v0:
```python
import jax
import jax.numpy as jnp
from jax import lax
from jax.sharding import PartitionSpec as P


def pair_list(levels):
    return [(low, high) for low in range(levels) for high in range(low + 1, levels)]


def place_slots(product, target, row_count):
    places = lax.broadcasted_iota(jnp.int32, (row_count, target.shape[0]), 0)
    placing = (target[None, :] == places).astype(jnp.float32)
    return jnp.einsum("qk,krv->qrv", placing, product, precision=lax.Precision.HIGHEST)


def slot_products(picked, blocks):
    return jnp.einsum("krw,kwv->krv", picked, blocks, preferred_element_type=jnp.float32)


def solve_level(residual, inverse, mask):
    return mask * jnp.dot(
        residual.astype(jnp.bfloat16), inverse, preferred_element_type=jnp.float32
    )


def local(
    right_side,
    live_width,
    lower_inverse,
    upper_inverse,
    lower_blocks,
    lower_source,
    lower_target,
    upper_blocks,
    upper_source,
    upper_target,
):
    levels = right_side.shape[0]
    width = right_side.shape[-1]
    slots = lower_blocks.shape[3]
    grid_rows = lax.axis_size("prow")
    pairs = pair_list(levels)
    columns = lax.broadcasted_iota(jnp.int32, (levels, 1, width), 2)
    live_mask = (columns < live_width[:, 0, :, None]).astype(jnp.float32)
    block_shape = right_side.shape[3:]
    partial_value = [jnp.zeros((grid_rows,) + block_shape, jnp.float32) for level in range(levels)]
    forward = []
    for level in range(levels):
        residual = right_side[level, 0, 0]
        if level > 0:
            incoming = lax.psum_scatter(
                partial_value[level].astype(jnp.bfloat16), "prow", scatter_dimension=0, tiled=True
            ).astype(jnp.float32)
            residual = residual - incoming[0]
        solved = solve_level(residual, lower_inverse[level, 0, 0], live_mask[level])
        forward.append(solved)
        chosen = [index for index, pair in enumerate(pairs) if pair[0] == level]
        if chosen:
            rounded = solved.astype(jnp.bfloat16)[None]
            sources = jnp.concatenate([lower_source[index, 0, 0] for index in chosen])
            gathered = lax.all_gather(rounded, "pcol", axis=0, tiled=True)
            picked = jnp.take(gathered, sources, axis=0)
            for order, index in enumerate(chosen):
                group = picked[order * slots : (order + 1) * slots]
                target_level = pairs[index][1]
                product = slot_products(group, lower_blocks[index, 0, 0])
                partial_value[target_level] = partial_value[target_level] + place_slots(
                    product, lower_target[index, 0, 0], grid_rows
                )
    partial_value = [jnp.zeros((grid_rows,) + block_shape, jnp.float32) for level in range(levels)]
    backward = [None] * levels
    for level in reversed(range(levels)):
        residual = forward[level]
        if level < levels - 1:
            incoming = lax.psum_scatter(
                partial_value[level].astype(jnp.bfloat16), "prow", scatter_dimension=0, tiled=True
            ).astype(jnp.float32)
            residual = residual - incoming[0]
        solved = solve_level(residual, upper_inverse[level, 0, 0], live_mask[level])
        backward[level] = solved
        chosen = [index for index, pair in enumerate(pairs) if pair[1] == level]
        if chosen:
            rounded = solved.astype(jnp.bfloat16)[None]
            sources = jnp.concatenate([upper_source[index, 0, 0] for index in chosen])
            gathered = lax.all_gather(rounded, "pcol", axis=0, tiled=True)
            picked = jnp.take(gathered, sources, axis=0)
            for order, index in enumerate(chosen):
                group = picked[order * slots : (order + 1) * slots]
                target_level = pairs[index][0]
                product = slot_products(group, upper_blocks[index, 0, 0])
                partial_value[target_level] = partial_value[target_level] + place_slots(
                    product, upper_target[index, 0, 0], grid_rows
                )
    forward_out = jnp.stack(forward)[:, None, None]
    backward_out = jnp.stack(backward)[:, None, None]
    return (forward_out, backward_out)


def solution(mesh):
    placed = (
        P(None, "prow", "pcol", None, None),
        P(None, "prow", "pcol"),
        P(None, "prow", "pcol", None, None),
        P(None, "prow", "pcol", None, None),
        P(None, "prow", "pcol", None, None, None),
        P(None, "prow", "pcol", None),
        P(None, "prow", "pcol", None),
        P(None, "prow", "pcol", None, None, None),
        P(None, "prow", "pcol", None),
        P(None, "prow", "pcol", None),
    )
    return jax.shard_map(
        local,
        mesh=mesh,
        in_specs=placed,
        out_specs=(P(None, "prow", "pcol", None, None), P(None, "prow", "pcol", None, None)),
        check_vma=False,
    )
```

profile of v0, /device:TPU:1, one launch (start us, length us, event | category | flops | bytes accessed | tf_op | source)
XLA Modules:
  0.0 605.3 jit_solution(17003166575744072773)
XLA Ops:
  7.2 0.0 all-gather.9.cloned.1.call-start
  7.2 0.7 compare_convert_fusion
  7.9 1.7 fusion.91
  9.7 0.0 all-gather.9.cloned.1.call-update
  9.7 0.0 reduce-scatter.5.cloned.1.call-start
  9.7 0.7 slice_bitcast_fusion.8
  10.4 0.1 compare_and_fusion.3
  10.5 0.7 slice_bitcast_fusion.5
  11.2 83.1 %all-gather.9.cloned.1.call-done = bf16[2048,256]{1,0:T(8,128)(2,1)} async-done(((bf16[64,256]{1,0:T(8,128)(2,1)}), bf16[2048,256]{1,0:T(8,128)(2,1)}) %all-gather.9.cloned.1.call-update) | async-done | bytes 1048592 | tf_op jit(solution)/shard_map/all_gather | solution.py:62
  94.3 1.8 gather_fusion
  96.1 0.0 copy-start
  96.1 0.0 copy-start.2
  96.1 1.4 fusion.13
  97.5 0.8 convolution_convert_fusion
  98.3 1.0 copy.19
  99.2 0.0 reduce-scatter.5.cloned.1.call-update
  99.3 0.0 all-gather.11.cloned.1.call-start
  99.3 59.5 %reduce-scatter.5.cloned.1.call-done = bf16[1,64,256]{2,1,0:T(8,128)(2,1)} async-done(((bf16[16,64,256]{2,1,0:T(8,128)(2,1)}), bf16[1,64,256]{2,1,0:T(8,128)(2,1)}) %reduce-scatter.5.cloned.1.call-update) | async-done | bytes 32784 | tf_op jit(solution)/shard_map/reduce_scatter | solution.py:52
  158.8 1.5 fusion.92
  160.3 0.0 all-gather.11.cloned.1.call-update
  160.4 0.0 reduce-scatter.7.cloned.1.call-start
  160.4 0.7 compare_and_fusion.2
  161.1 1.3 fusion.11
  162.4 0.8 fusion.28
  163.2 77.7 %all-gather.11.cloned.1.call-done = bf16[2048,256]{1,0:T(8,128)(2,1)} async-done(((bf16[64,256]{1,0:T(8,128)(2,1)}), bf16[2048,256]{1,0:T(8,128)(2,1)}) %all-gather.11.cloned.1.call-update) | async-done | bytes 1048592 | tf_op jit(solution)/shard_map/all_gather | solution.py:62
  240.9 1.8 gather_fusion.1
  242.7 1.3 fusion.9
  244.0 0.0 copy-start.1
  244.0 0.0 copy-start.5
  244.0 0.8 fusion
  244.8 0.0 copy-start.3
  244.8 1.0 copy.20
  245.8 0.0 reduce-scatter.7.cloned.1.call-update
  245.8 0.0 all-gather.13.cloned.1.call-start
  245.9 59.6 %reduce-scatter.7.cloned.1.call-done = bf16[1,64,256]{2,1,0:T(8,128)(2,1)} async-done(((bf16[16,64,256]{2,1,0:T(8,128)(2,1)}), bf16[1,64,256]{2,1,0:T(8,128)(2,1)}) %reduce-scatter.7.cloned.1.call-update) | async-done | bytes 32784 | tf_op jit(solution)/shard_map/reduce_scatter | solution.py:52
  305.5 0.9 convolution_multiply_fusion.3
  306.4 0.0 copy-done.1
  306.4 0.8 fusion.93
  307.2 0.0 all-gather.13.cloned.1.call-update
  307.2 0.0 reduce-scatter.9.cloned.1.call-start
  307.3 0.1 compare_and_fusion.1
  307.4 79.4 %all-gather.13.cloned.1.call-done = bf16[2048,256]{1,0:T(8,128)(2,1)} async-done(((bf16[64,256]{1,0:T(8,128)(2,1)}), bf16[2048,256]{1,0:T(8,128)(2,1)}) %all-gather.13.cloned.1.call-update) | async-done | bytes 1048592 | tf_op jit(solution)/shard_map/all_gather | solution.py:86
  386.8 1.8 gather_fusion.2
  388.6 0.2 fusion.5
  388.9 0.8 fusion.23
  389.7 1.0 copy.49
  390.7 0.0 reduce-scatter.9.cloned.1.call-update
  390.7 0.0 all-gather.15.cloned.1.call-start
  390.7 59.6 %reduce-scatter.9.cloned.1.call-done = bf16[1,64,256]{2,1,0:T(8,128)(2,1)} async-done(((bf16[16,64,256]{2,1,0:T(8,128)(2,1)}), bf16[1,64,256]{2,1,0:T(8,128)(2,1)}) %reduce-scatter.9.cloned.1.call-update) | async-done | bytes 32784 | tf_op jit(solution)/shard_map/reduce_scatter | solution.py:76
  450.4 1.5 fusion.94
  451.9 0.0 all-gather.15.cloned.1.call-update
  451.9 0.0 reduce-scatter.11.cloned.1.call-start
  452.0 0.2 fusion.7
  452.3 0.8 fusion.25
  453.1 79.3 %all-gather.15.cloned.1.call-done = bf16[2048,256]{1,0:T(8,128)(2,1)} async-done(((bf16[64,256]{1,0:T(8,128)(2,1)}), bf16[2048,256]{1,0:T(8,128)(2,1)}) %all-gather.15.cloned.1.call-update) | async-done | bytes 1048592 | tf_op jit(solution)/shard_map/all_gather | solution.py:86
  532.3 1.8 gather_fusion.3
  534.1 0.2 fusion.3
  534.4 0.8 fusion.21
  535.2 1.9 fusion.2
  537.1 0.0 reduce-scatter.11.cloned.1.call-update
  537.1 0.7 maximum_bitcast_fusion
  537.8 59.0 %reduce-scatter.11.cloned.1.call-done = bf16[1,64,256]{2,1,0:T(8,128)(2,1)} async-done(((bf16[16,64,256]{2,1,0:T(8,128)(2,1)}), bf16[1,64,256]{2,1,0:T(8,128)(2,1)}) %reduce-scatter.11.cloned.1.call-update) | async-done | bytes 32784 | tf_op jit(solution)/shard_map/reduce_scatter | solution.py:76
  596.8 0.9 fusion.1
  597.7 0.7 maximum_bitcast_fusion.1
  (14 shorter events, 0.1 us)
Async XLA Ops:
  7.2 87.1 %all-gather.9.cloned.1.call-start = ((), (), s32[]{:S(2)}) async-start(), calls=%async_computation.8 | async-start | bytes 1081344 | tf_op jit(solution)/shard_map/all_gather | solution.py:62
  9.7 149.1 %reduce-scatter.5.cloned.1.call-start = ((), (), s32[]{:S(2)}) async-start(), calls=%async_computation.4 | async-start | bytes 557056 | tf_op jit(solution)/shard_map/reduce_scatter | solution.py:52
  96.1 62.7 %copy-start = (bf16[3,1,1,256,256]{4,3,2,1,0:T(8,128)(2,1)S(1)}, bf16[3,1,1,256,256]{4,3,2,1,0:T(8,128)(2,1)}, u32[]{:S(2)}) copy-start(bf16[3,1,1,256,256]{4,3,2,1,0:T(8,128)(2,1)} %param.16) | copy-start | bytes 1179652
  96.1 62.7 %copy-start.2 = (f32[3,1,1,64,256]{4,3,2,1,0:T(8,128)S(1)}, f32[3,1,1,64,256]{4,3,2,1,0:T(8,128)}, u32[]{:S(2)}) copy-start(f32[3,1,1,64,256]{4,3,2,1,0:T(8,128)} %param.14) | copy-start | bytes 589828
  99.3 141.6 %all-gather.11.cloned.1.call-start = ((), (), s32[]{:S(2)}) async-start(), calls=%async_computation.9 | async-start | bytes 1081344 | tf_op jit(solution)/shard_map/all_gather | solution.py:62
  160.4 145.2 %reduce-scatter.7.cloned.1.call-start = ((), (), s32[]{:S(2)}) async-start(), calls=%async_computation.5 | async-start | bytes 557056 | tf_op jit(solution)/shard_map/reduce_scatter | solution.py:52
  244.0 62.4 %copy-start.1 = (bf16[3,1,1,256,256]{4,3,2,1,0:T(8,128)(2,1)S(1)}, bf16[3,1,1,256,256]{4,3,2,1,0:T(8,128)(2,1)}, u32[]{:S(2)}) copy-start(bf16[3,1,1,256,256]{4,3,2,1,0:T(8,128)(2,1)} %param.17) | copy-start | bytes 1179652
  244.0 63.3 %copy-start.5 = (s32[3,1,1,4]{3,2,1,0:T(1,128)S(1)}, s32[3,1,1,4]{3,2,1,0:T(1,128)}, u32[]{:S(2)}) copy-start(s32[3,1,1,4]{3,2,1,0:T(1,128)} %param.22) | copy-start | bytes 148
  244.0 63.4 %copy-start.4 = (s32[3,1,1,4]{3,2,1,0:T(1,128)S(1)}, s32[3,1,1,4]{3,2,1,0:T(1,128)}, u32[]{:S(2)}) copy-start(s32[3,1,1,4]{3,2,1,0:T(1,128)} %param.23) | copy-start | bytes 148
  244.8 143.8 %copy-start.3 = (bf16[3,1,1,4,256,256]{5,4,3,2,1,0:T(8,128)(2,1)S(1)}, bf16[3,1,1,4,256,256]{5,4,3,2,1,0:T(8,128)(2,1)}, u32[]{:S(2)}) copy-start(bf16[3,1,1,4,256,256]{5,4,3,2,1,0:T(8,128)(2,1)} %param.21) | copy-start | bytes 4718596
  245.8 141.0 %all-gather.13.cloned.1.call-start = ((), (), s32[]{:S(2)}) async-start(), calls=%async_computation.10 | async-start | bytes 1081344 | tf_op jit(solution)/shard_map/all_gather | solution.py:86
  307.2 143.1 %reduce-scatter.9.cloned.1.call-start = ((), (), s32[]{:S(2)}) async-start(), calls=%async_computation.6 | async-start | bytes 557056 | tf_op jit(solution)/shard_map/reduce_scatter | solution.py:76
  390.7 141.6 %all-gather.15.cloned.1.call-start = ((), (), s32[]{:S(2)}) async-start(), calls=%async_computation.11 | async-start | bytes 1081344 | tf_op jit(solution)/shard_map/all_gather | solution.py:86
  451.9 144.9 %reduce-scatter.11.cloned.1.call-start = ((), (), s32[]{:S(2)}) async-start(), calls=%async_computation.7 | async-start | bytes 557056 | tf_op jit(solution)/shard_map/reduce_scatter | solution.py:76
Sparse Core Ops, SparseCore 0:
  11.7 82.5 all-gather.8
  99.4 59.3 reduce-scatter.4
  163.0 77.8 all-gather.10
  245.9 59.5 reduce-scatter.6
  309.1 77.6 all-gather.12
  390.8 59.5 reduce-scatter.8
  454.6 77.6 all-gather.14
  537.3 59.5 reduce-scatter.10
where the time goes:
time: 608 us; the launch traced here: 605 us
  waiting for transfers between devices  557 us (92%)
  matrix products  16.8 us (3%)
  between operations  14.4 us (2%)
  local copies, waits for them, and re-layouts  11.5 us (2%)
    all_gather x4, waiting for transfers between devices, local(): gathered = lax.all_gather(rounded, 'pcol', axis=0, tiled=True)  320 us
    reduce_scatter x4, waiting for transfers between devices, local(): lax.psum_scatter(partial_value[level].astype(jnp.bfloat16), 'prow', scatt...  238 us
  transfers between devices with their start and end apart: 8, of which 8 were waited for; matrix products, arithmetic and copies ran while one was open for 1% of the time, Pallas kernels for 0%

commit v1 on v0

v1 whole, which is shorter than its diff:
```python
import functools

import jax
import jax.numpy as jnp
from jax import lax
from jax.experimental import pallas as pl
from jax.experimental.pallas import tpu as pltpu
from jax.sharding import PartitionSpec as P


MESH = pl.DeviceIdType.MESH
NX = 4
CORES = 2
ROWS = 16
LANES = 128
SLOTS = 4
BF16 = jnp.bfloat16
F32 = jnp.float32
LOW_SOURCE, LOW_TARGET, UP_SOURCE, UP_TARGET, LIVE = 0, 12, 24, 36, 48


def kernel(
    ny,
    nz,
    rhs,
    live_width,
    low_source,
    low_target,
    up_source,
    up_target,
    inv_low,
    inv_up,
    blk_low,
    blk_up,
    out_f,
    out_b,
    rhs_first,
    rhs_rest,
    w_inv_low,
    w_inv_up,
    w_low,
    w_up,
    x_first,
    xf,
    yb,
    piece,
    held,
    stage,
    pick,
    prod,
    acc,
    part,
    landed,
    tabs,
    stab,
    local_sem,
    pair_send,
    pair_recv,
    tab_send,
    tab_recv,
    tab_local,
    spread_send,
    spread_recv,
    pick_send,
    pick_recv,
    sum_send,
    sum_recv,
    out_local,
    out_send,
    out_recv,
):
    prow, pcol = lax.axis_index("prow"), lax.axis_index("pcol")
    z, c = prow // CORES, prow % CORES
    y, x = pcol // NX, pcol % NX
    other = 1 - c
    n_plane = ny * NX

    def at(zz, cc, yy, xx):
        return {"prow": zz * CORES + cc, "pcol": yy * NX + xx}

    def remote(src, dst, send, recv, where):
        return pltpu.make_async_remote_copy(
            src_ref=src, dst_ref=dst, send_sem=send, recv_sem=recv, device_id=where, device_id_type=MESH
        )

    partner = at(z, other, y, x)
    mine = pl.ds(pl.multiple_of(c * 2 * ROWS, 2 * ROWS), 2 * ROWS)
    theirs = pl.ds(pl.multiple_of(other * 2 * ROWS, 2 * ROWS), 2 * ROWS)

    first_rhs = pltpu.make_async_copy(rhs.at[0], rhs_first, local_sem.at[0])
    first_inv = pltpu.make_async_copy(inv_low.at[0], w_inv_low.at[0, 0], local_sem.at[1])
    first_rhs.start()
    first_inv.start()
    own = []
    shared = []

    def both(src, dst_own, dst_partner, src_partner=None):
        n = len(own)
        own.append(pltpu.make_async_copy(src, dst_own, local_sem.at[2 + n]))
        own[-1].start()
        shared.append(
            remote(src if src_partner is None else src_partner, dst_partner, pair_send.at[1 + n], pair_recv.at[1 + n], partner)
        )
        return n

    got = {}
    got["low", 0] = both(blk_low.at[0], w_low.at[0, 0], w_low.at[0, 1])
    got["low", 1] = both(blk_low.at[1], w_low.at[1, 0], w_low.at[1, 1])
    got["rhs"] = both(rhs.at[pl.ds(1, 2), mine], rhs_rest.at[0], rhs_rest.at[1], rhs.at[pl.ds(1, 2), theirs])
    got["inv_low"] = both(inv_low.at[pl.ds(1, 2)], w_inv_low.at[pl.ds(1, 2), 0], w_inv_low.at[pl.ds(1, 2), 1])
    got["low", 2] = both(blk_low.at[2], w_low.at[2, 0], w_low.at[2, 1])
    got["inv_up"] = both(inv_up, w_inv_up.at[:, 0], w_inv_up.at[:, 1])
    got["up", 2] = both(blk_up.at[2], w_up.at[2, 0], w_up.at[2, 1])
    got["up", 1] = both(blk_up.at[1], w_up.at[1, 0], w_up.at[1, 1])
    got["up", 0] = both(blk_up.at[0], w_up.at[0, 0], w_up.at[0, 1])

    spot = lax.broadcasted_iota(jnp.int32, (8, LANES), 1)
    row = jnp.zeros((8, LANES), jnp.int32)
    for base, small in ((LOW_SOURCE, low_source), (LOW_TARGET, low_target), (UP_SOURCE, up_source), (UP_TARGET, up_target)):
        for pair in range(3):
            for k in range(SLOTS):
                row = jnp.where(spot == base + SLOTS * pair + k, small[pair, 0, 0, k], row)
    for level in range(3):
        row = jnp.where(spot == LIVE + level, live_width[level], row)
    tabs[0, x] = row

    def need(name):
        own[got[name]].wait()
        shared[got[name]].wait_recv()

    barrier = pltpu.get_barrier_semaphore()

    def hello(where):
        pl.semaphore_signal(barrier, inc=1, device_id=where, device_id_type=MESH)

    def far(index, count):
        step = (index + 1) // 2
        return count // 2 + step * (1 - 2 * (index % 2))

    def plane_loop(act):
        def row(i, carry):
            yy = lax.rem(y + far(i, ny), ny)
            for dx in (2, 1, 3, 0):
                act(yy, lax.rem(x + dx, NX))
            return carry

        lax.fori_loop(0, ny - 1, row, 0)
        for dx in (2, 1, 3):
            act(y, lax.rem(x + dx, NX))

    plane_loop(lambda yy, xx: hello(at(z, c, yy, xx)))

    def hello_z(i, carry):
        hello(at(lax.rem(z + far(i, nz), nz), c, y, x))
        return carry

    lax.fori_loop(0, nz - 1, hello_z, 0)
    for dx in range(NX):
        hello(at(z, other, y, lax.rem(x + dx, NX)))

    lane = lax.broadcasted_iota(jnp.int32, (1, 2 * LANES), 1)

    def live_mask(width):
        return (lane < width).astype(F32)

    def dot(left, right):
        return jnp.dot(left, right, preferred_element_type=F32)

    first_rhs.wait()
    first_inv.wait()
    x_first[...] = live_mask(live_width[0]) * dot(rhs_first[...].astype(BF16), w_inv_low[0, 0])
    xf[0, 0] = x_first[mine, :]
    first_out = pltpu.make_async_copy(x_first, out_f.at[0], out_local.at[0])
    first_out.start()

    pl.semaphore_wait(barrier, (n_plane - 1) + (nz - 1) + NX)
    first_x = remote(x_first.at[theirs], xf.at[0, 1], pair_send.at[0], pair_recv.at[0], partner)
    first_x.start()

    tab_copies = []
    for a in range(CORES):
        for dx in range(NX):
            if (a, dx) != (0, 0):
                tab_copies.append(
                    remote(
                        tabs.at[0, x],
                        tabs.at[a, x],
                        tab_send.at[len(tab_copies)],
                        tab_recv.at[len(tab_copies)],
                        at(z, c if a == 0 else other, y, lax.rem(x + dx, NX)),
                    )
                )
                tab_copies[-1].start()
    for copy in shared[:2]:
        copy.start()

    me = y * NX + x

    def spread(t, r, values):
        for a in range(CORES):
            rounded = values[a].astype(BF16)
            for h in range(2):
                piece[t, r, 2 * a + h] = rounded[:, h * LANES : (h + 1) * LANES]

        def send(yy, xx):
            remote(
                piece.at[t, r, xx], held[2 * t + r].at[me], spread_send.at[t, r], spread_recv.at[t, r], at(z, c, yy, xx)
            ).start()

        plane_loop(send)
        held[2 * t + r][me] = piece[t, r, x]

    def spread_done(t, r):
        span = held[2 * t + r].at[pl.ds(0, n_plane - 1)]
        remote(span, span, spread_send.at[t, r], spread_recv.at[t, r], partner).wait_recv()

    def choose(t, r, n, base):
        a = x // 2
        for d in (2, 1, 3, 0):
            xx = lax.rem(x + d, NX)
            for k in range(SLOTS):
                tile = held[2 * t + r][stab[a, xx, 0, base + k]]
                if d:
                    stage[t, r, n, d - 1, k] = tile
                else:
                    pick[t, r, n, x, k] = tile
            if d:
                remote(
                    stage.at[t, r, n, d - 1], pick.at[t, r, n, x], pick_send.at[t, r, n], pick_recv.at[t, r, n], at(z, c, y, xx)
                ).start()

    def choose_done(t, r, n):
        span = pick.at[t, r, n, pl.ds(0, NX - 1)]
        remote(span, span, pick_send.at[t, r, n], pick_recv.at[t, r, n], partner).wait_recv()

    def products(t, r, n, weights, pair):
        for a in range(CORES):
            for k in range(SLOTS):
                left = jnp.concatenate([pick[t, r, n, 2 * a, k], pick[t, r, n, 2 * a + 1, k]], axis=1)
                prod[a * SLOTS + k] = dot(left, weights[pair, a, k])

    def placed(base, q):
        total = None
        for a in range(CORES):
            for k in range(SLOTS):
                hit = jnp.where(stab[a, x, 0, base + k] == q, 1.0, 0.0).astype(F32)
                term = prod[a * SLOTS + k] * hit
                total = term if total is None else total + term
        return total

    def target_of(d, a):
        return CORES * lax.rem(z + d, nz) + (c if a == 0 else other)

    def keep(r, base):
        def one(d, carry):
            for a in range(CORES):
                acc[r, d, a] = placed(base, target_of(d, a))
            return carry

        lax.fori_loop(0, nz, one, 0)

    def exchange(t, r, base, with_kept):
        def value(d, a):
            total = placed(base, target_of(d, a))
            return total + acc[r, d, a] if with_kept else total

        def one(i, carry):
            d = far(i, nz)
            for a in range(CORES):
                part[t, r, d - 1, a] = value(d, a).astype(BF16)
            remote(
                part.at[t, r, d - 1],
                landed.at[t, r, d - 1],
                sum_send.at[t, r],
                sum_recv.at[t, r],
                at(lax.rem(z + d, nz), c, y, x),
            ).start()
            return carry

        lax.fori_loop(0, nz - 1, one, 0)
        return [value(0, a) for a in range(CORES)]

    def summed(t, r, kept):
        remote(landed.at[t, r], landed.at[t, r], sum_send.at[t, r], sum_recv.at[t, r], partner).wait_recv()
        totals = []
        for a in range(CORES):
            total = kept[a]
            for d in range(nz - 1):
                total = total + landed[t, r, d, a].astype(F32)
            totals.append(total)
        return totals

    masks = {}

    def mask(level, a):
        if (level, a) not in masks:
            masks[level, a] = live_mask(stab[a, x, 0, LIVE + level])
        return masks[level, a]

    def solve(level, weights, residual):
        return [mask(level, a) * dot(residual[a].astype(BF16), weights[level, a]) for a in range(CORES)]

    def rows(r):
        return slice(r * ROWS, (r + 1) * ROWS)

    out_copies = []

    def put(out, values, level):
        n = len(out_copies) // 2
        out_copies.append(pltpu.make_async_copy(values.at[level, 0], out.at[level, mine], out_local.at[1 + n]))
        out_copies.append(remote(values.at[level, 1], out.at[level, mine], out_send.at[n], out_recv.at[n], partner))
        out_copies[-2].start()
        out_copies[-1].start()

    chunks = range(2)

    first_x.wait_recv()
    for r in chunks:
        spread(0, r, [xf[0, a, rows(r)] for a in range(CORES)])
    for copy in shared[2:]:
        copy.start()
    for copy in tab_copies:
        copy.wait_recv()
    to_scalar = pltpu.make_async_copy(tabs, stab, tab_local)
    to_scalar.start()
    to_scalar.wait()

    def round_of(t, weights, name, base_source, base_target, crit, late, with_kept):
        for r in chunks:
            spread_done(t, r)
            choose(t, r, 0, base_source + SLOTS * crit)
        if late is not None:
            for r in chunks:
                choose(t, r, 1, base_source + SLOTS * late)
        kept = []
        need((name, crit))
        for r in chunks:
            choose_done(t, r, 0)
            products(t, r, 0, weights, crit)
            kept.append(exchange(t, r, base_target + SLOTS * crit, with_kept))
        if late is not None:
            need((name, late))
            for r in chunks:
                choose_done(t, r, 1)
                products(t, r, 1, weights, late)
                keep(r, base_target + SLOTS * late)
        return kept

    kept = round_of(0, w_low, "low", LOW_SOURCE, LOW_TARGET, 0, 1, False)
    need("rhs")
    need("inv_low")
    for r in chunks:
        total = summed(0, r, kept[r])
        solved = solve(1, w_inv_low, [rhs_rest[a, 0, rows(r)] - total[a] for a in range(CORES)])
        spread(1, r, solved)
        for a in range(CORES):
            xf[1, a, rows(r)] = solved[a]
    put(out_f, xf, 1)

    kept = round_of(1, w_low, "low", LOW_SOURCE, LOW_TARGET, 2, None, True)
    need("inv_up")
    for r in chunks:
        total = summed(1, r, kept[r])
        solved = solve(2, w_inv_low, [rhs_rest[a, 1, rows(r)] - total[a] for a in range(CORES)])
        back = solve(2, w_inv_up, solved)
        spread(2, r, back)
        for a in range(CORES):
            xf[2, a, rows(r)] = solved[a]
            yb[2, a, rows(r)] = back[a]
    put(out_f, xf, 2)
    put(out_b, yb, 2)

    kept = round_of(2, w_up, "up", UP_SOURCE, UP_TARGET, 2, 1, False)
    for r in chunks:
        total = summed(2, r, kept[r])
        back = solve(1, w_inv_up, [xf[1, a, rows(r)] - total[a] for a in range(CORES)])
        spread(3, r, back)
        for a in range(CORES):
            yb[1, a, rows(r)] = back[a]
    put(out_b, yb, 1)

    kept = round_of(3, w_up, "up", UP_SOURCE, UP_TARGET, 0, None, True)
    for r in chunks:
        total = summed(3, r, kept[r])
        back = solve(0, w_inv_up, [xf[0, a, rows(r)] - total[a] for a in range(CORES)])
        for a in range(CORES):
            yb[0, a, rows(r)] = back[a]
    put(out_b, yb, 0)

    first_out.wait()
    first_x.wait_send()
    for copy in shared + tab_copies:
        copy.wait_send()
    for t in range(4):
        for r in chunks:
            span = held[2 * t + r].at[pl.ds(0, n_plane - 1)]
            remote(span, span, spread_send.at[t, r], spread_recv.at[t, r], partner).wait_send()
            for n in range(2 if t % 2 == 0 else 1):
                span = pick.at[t, r, n, pl.ds(0, NX - 1)]
                remote(span, span, pick_send.at[t, r, n], pick_recv.at[t, r, n], partner).wait_send()
            remote(landed.at[t, r], landed.at[t, r], sum_send.at[t, r], sum_recv.at[t, r], partner).wait_send()
    for copy in out_copies:
        copy.wait()


def deliver(forward, backward, out_f, out_b, sem):
    copies = [
        pltpu.make_async_copy(src.at[level], dst.at[level], sem.at[n, level])
        for n, (src, dst) in enumerate(((forward, out_f), (backward, out_b)))
        for level in range(3)
    ]
    for copy in copies:
        copy.start()
    for copy in copies:
        copy.wait()


def local(
    ny,
    nz,
    right_side,
    live_width,
    lower_inverse,
    upper_inverse,
    lower_blocks,
    lower_source,
    lower_target,
    upper_blocks,
    upper_source,
    upper_target,
):
    levels, _, _, count, width = right_side.shape
    n_plane = ny * NX
    dma = pltpu.SemaphoreType.DMA
    hbm = pl.BlockSpec(memory_space=pl.ANY)
    out = jax.ShapeDtypeStruct((levels, count, width), F32)
    forward, backward = pl.pallas_call(
        functools.partial(kernel, ny, nz),
        out_shape=(pltpu.VMEM(out.shape, F32), pltpu.VMEM(out.shape, F32)),
        in_specs=[hbm] + [pl.BlockSpec(memory_space=pltpu.SMEM)] * 5 + [hbm] * 4,
        out_specs=(hbm, hbm),
        scratch_shapes=[
            pltpu.VMEM((count, width), F32),
            pltpu.VMEM((CORES, levels - 1, 2 * ROWS, width), F32),
            pltpu.VMEM((levels, CORES, width, width), BF16),
            pltpu.VMEM((levels, CORES, width, width), BF16),
            pltpu.VMEM((levels, CORES, SLOTS, width, width), BF16),
            pltpu.VMEM((levels, CORES, SLOTS, width, width), BF16),
            pltpu.VMEM((count, width), F32),
            pltpu.VMEM((levels, CORES, 2 * ROWS, width), F32),
            pltpu.VMEM((levels, CORES, 2 * ROWS, width), F32),
            pltpu.VMEM((4, 2, NX, ROWS, LANES), BF16),
            [pltpu.VMEM((n_plane, ROWS, LANES), BF16) for _ in range(8)],
            pltpu.VMEM((4, 2, 2, NX - 1, SLOTS, ROWS, LANES), BF16),
            pltpu.VMEM((4, 2, 2, NX, SLOTS, ROWS, LANES), BF16),
            pltpu.VMEM((CORES * SLOTS, ROWS, width), F32),
            pltpu.VMEM((2, nz, CORES, ROWS, width), F32),
            pltpu.VMEM((4, 2, nz - 1, CORES, ROWS, width), BF16),
            pltpu.VMEM((4, 2, nz - 1, CORES, ROWS, width), BF16),
            pltpu.VMEM((CORES, NX, 8, LANES), jnp.int32),
            pltpu.SMEM((CORES, NX, 8, LANES), jnp.int32),
            dma((11,)),
            dma((10,)),
            dma((10,)),
            dma((7,)),
            dma((7,)),
            dma(()),
            dma((4, 2)),
            dma((4, 2)),
            dma((4, 2, 2)),
            dma((4, 2, 2)),
            dma((4, 2)),
            dma((4, 2)),
            dma((6,)),
            dma((5,)),
            dma((5,)),
        ],
        compiler_params=pltpu.CompilerParams(collective_id=0, has_side_effects=True, vmem_limit_bytes=60 << 20),
        cost_estimate=pl.CostEstimate(flops=252 << 20, bytes_accessed=8 << 20, transcendentals=0),
    )(
        right_side.reshape(levels, count, width),
        live_width.reshape(levels),
        lower_source,
        lower_target,
        upper_source,
        upper_target,
        lower_inverse.reshape(levels, width, width),
        upper_inverse.reshape(levels, width, width),
        lower_blocks.reshape(levels, SLOTS, width, width),
        upper_blocks.reshape(levels, SLOTS, width, width),
    )
    forward, backward = pl.pallas_call(
        deliver,
        out_shape=(out, out),
        in_specs=[pl.BlockSpec(memory_space=pltpu.VMEM), pl.BlockSpec(memory_space=pltpu.VMEM)],
        out_specs=(hbm, hbm),
        scratch_shapes=[dma((2, 3))],
        compiler_params=pltpu.CompilerParams(vmem_limit_bytes=1 << 20),
        cost_estimate=pl.CostEstimate(flops=0, bytes_accessed=1 << 20, transcendentals=0),
    )(forward, backward)
    return forward[:, None, None], backward[:, None, None]


def solution(mesh):
    placed = (
        P(None, "prow", "pcol", None, None),
        P(None, "prow", "pcol"),
        P(None, "prow", "pcol", None, None),
        P(None, "prow", "pcol", None, None),
        P(None, "prow", "pcol", None, None, None),
        P(None, "prow", "pcol", None),
        P(None, "prow", "pcol", None),
        P(None, "prow", "pcol", None, None, None),
        P(None, "prow", "pcol", None),
        P(None, "prow", "pcol", None),
    )
    return jax.shard_map(
        functools.partial(local, mesh.shape["pcol"] // NX, mesh.shape["prow"] // CORES),
        mesh=mesh,
        in_specs=placed,
        out_specs=(P(None, "prow", "pcol", None, None), P(None, "prow", "pcol", None, None)),
        check_vma=False,
    )
```

time: 608 us -> 87 us (0.14)
  waiting for transfers between devices: 557 us -> 0 us
  Pallas kernels: 0 us -> 86.3 us
  matrix products: 16.8 us -> 0 us
  between operations: 14.4 us -> 0.64 us
  local copies, waits for them, and re-layouts: 11.5 us -> 0 us
    all_gather x4 -> x0, waiting for transfers between devices: 320 us -> none  [local(): gathered = lax.all_gather(rounded, 'pcol', axis=0, tiled=True)]
    reduce_scatter x4 -> x0, waiting for transfers between devices: 238 us -> none  [local(): lax.psum_scatter(partial_value[level].astype(jnp.bfloat16), 'prow', scatt...]
    pallas_call x0 -> x2, Pallas kernels: none -> 86.3 us  [the longest x1 85.5 us: local(): pl.pallas_call(functools.partial(kernel, ny, nz), out_shape=(pltpu.VMEM(o...]
    dot_general x18 -> x0, matrix products: 16.8 us -> none  [the longest x6 7.34 us: solve_level(): jnp.dot(residual.astype(jnp.bfloat16), inverse, preferred_element_type=jn...]
    gather x4 -> x0, local copies, waits for them, and re-layouts: 7.13 us -> none  [local(): picked = jnp.take(gathered, sources, axis=0)]
  transfers between devices with their start and end apart: 8 -> 0, of which waited for: 8 -> 0; matrix products, arithmetic and copies ran while one was open for 1% -> 0% of each run, Pallas kernels for 0% -> 0%
where the time goes in v1:
time: 87 us; the launch traced here: 86.9 us
  Pallas kernels  86.3 us (99%)
    pallas_call x1, Pallas kernels, local(): pl.pallas_call(functools.partial(kernel, ny, nz), out_shape=(pltpu.VMEM(o...  85.5 us

profile of v1, /device:TPU:1, one launch (start us, length us, event | category | flops | bytes accessed | tf_op | source)
XLA Modules:
  0.0 86.9 jit_solution(2883815151726188656)
XLA Ops:
  0.6 85.5 %shard_map.113 = (f32[3,64,256]{2,1,0:T(8,128)S(1)}, f32[3,64,256]{2,1,0:T(8,128)S(1)}) custom-call(f32[3,64,256]{2,1,0:T(8,128)} %bitcast.16, s32[3]{0:T(128)} %bitcast.17, s32[3,1,1,4]{3,2,1,0:T(1,128)} %low_source.1, s32[3,1,1,4]{3,2,1,0:T(1,128)} %low_target.1, s32[3,1,1,4]{3,2,1,0:T(1,128)} %up_source.1, s32[3,1,1,4]{3,2,1,0:T(1,128)} %up_target.1, ...), custom_call_target="tpu_custom_call" | custom-call | flops 264241152 | bytes 8388608 | tf_op jit(solution)/shard_map/pallas_call | solution.py:437
  86.1 0.8 shard_map.114

commit v2 on v1

v2 whole, which is shorter than its diff:
```python
import functools

import jax
import jax.numpy as jnp
from jax import lax
from jax.experimental import pallas as pl
from jax.experimental.pallas import tpu as pltpu
from jax.sharding import PartitionSpec as P


MESH = pl.DeviceIdType.MESH
NX = 4
CORES = 2
CHUNKS = 4
PART = 8
ROWS = CORES * PART
LANES = 128
SLOTS = 4
BF16 = jnp.bfloat16
F32 = jnp.float32
LOW_SOURCE, LOW_TARGET, UP_SOURCE, UP_TARGET, LIVE = 0, 12, 24, 36, 48


def kernel(
    ny,
    nz,
    rhs,
    live_width,
    low_source,
    low_target,
    up_source,
    up_target,
    inv_low,
    inv_up,
    blk_low,
    blk_up,
    out_f,
    out_b,
    rhs_first,
    rhs_rest,
    w_inv_low,
    w_inv_up,
    w_low,
    w_up,
    x_first,
    xf,
    yb,
    piece,
    held,
    stage,
    pick,
    prod,
    acc,
    mine_sum,
    part,
    landed,
    tabs,
    stab,
    local_sem,
    pair_send,
    pair_recv,
    tab_send,
    tab_recv,
    tab_local,
    spread_send,
    spread_recv,
    pick_send,
    pick_recv,
    sum_send,
    sum_recv,
    out_local,
    out_send,
    out_recv,
):
    prow, pcol = lax.axis_index("prow"), lax.axis_index("pcol")
    z, c = prow // CORES, prow % CORES
    y, x = pcol // NX, pcol % NX
    other = 1 - c

    def at(zz, cc, yy, xx):
        return {"prow": zz * CORES + cc, "pcol": yy * NX + xx}

    def remote(src, dst, send, recv, where):
        return pltpu.make_async_remote_copy(
            src_ref=src, dst_ref=dst, send_sem=send, recv_sem=recv, device_id=where, device_id_type=MESH
        )

    partner = at(z, other, y, x)
    mine = pl.ds(pl.multiple_of(c * CHUNKS * PART, CHUNKS * PART), CHUNKS * PART)
    theirs = pl.ds(pl.multiple_of(other * CHUNKS * PART, CHUNKS * PART), CHUNKS * PART)

    barrier = pltpu.get_barrier_semaphore()

    def hello(where):
        pl.semaphore_signal(barrier, inc=1, device_id=where, device_id_type=MESH)

    def far(index, count):
        step = (index + 1) // 2
        return count // 2 + step * (1 - 2 * (index % 2))

    def ring(act, count):
        def one(i, carry):
            act(far(i, count))
            return carry

        lax.fori_loop(0, count - 1, one, 0)

    ring(lambda d: hello(at(z, c, lax.rem(y + d, ny), x)), ny)
    ring(lambda d: hello(at(lax.rem(z + d, nz), c, y, x)), nz)
    for dx in range(1, NX):
        hello(at(z, c, y, lax.rem(x + dx, NX)))
    for dx in range(NX):
        hello(at(z, other, y, lax.rem(x + dx, NX)))

    first_rhs = pltpu.make_async_copy(rhs.at[0], rhs_first, local_sem.at[0])
    first_inv = pltpu.make_async_copy(inv_low.at[0], w_inv_low.at[0, 0], local_sem.at[1])
    first_rhs.start()
    first_inv.start()
    own = []
    shared = []

    def both(src, dst_own, dst_partner, src_partner=None):
        n = len(own)
        own.append(pltpu.make_async_copy(src, dst_own, local_sem.at[2 + n]))
        own[-1].start()
        shared.append(
            remote(src if src_partner is None else src_partner, dst_partner, pair_send.at[1 + n], pair_recv.at[1 + n], partner)
        )
        return n

    got = {}
    got["low", 0] = both(blk_low.at[0], w_low.at[0, 0], w_low.at[0, 1])
    got["low", 1] = both(blk_low.at[1], w_low.at[1, 0], w_low.at[1, 1])
    got["rhs"] = both(rhs.at[pl.ds(1, 2), mine], rhs_rest.at[0], rhs_rest.at[1], rhs.at[pl.ds(1, 2), theirs])
    got["inv_low"] = both(inv_low.at[pl.ds(1, 2)], w_inv_low.at[pl.ds(1, 2), 0], w_inv_low.at[pl.ds(1, 2), 1])
    got["low", 2] = both(blk_low.at[2], w_low.at[2, 0], w_low.at[2, 1])
    got["inv_up"] = both(inv_up, w_inv_up.at[:, 0], w_inv_up.at[:, 1])
    got["up", 2] = both(blk_up.at[2], w_up.at[2, 0], w_up.at[2, 1])
    got["up", 1] = both(blk_up.at[1], w_up.at[1, 0], w_up.at[1, 1])
    got["up", 0] = both(blk_up.at[0], w_up.at[0, 0], w_up.at[0, 1])

    spot = lax.broadcasted_iota(jnp.int32, (8, LANES), 1)
    row = jnp.zeros((8, LANES), jnp.int32)
    for base, small in ((LOW_SOURCE, low_source), (LOW_TARGET, low_target), (UP_SOURCE, up_source), (UP_TARGET, up_target)):
        for pair in range(3):
            for k in range(SLOTS):
                row = jnp.where(spot == base + SLOTS * pair + k, small[pair, 0, 0, k], row)
    for level in range(3):
        row = jnp.where(spot == LIVE + level, live_width[level], row)
    tabs[0, x] = row

    def need(name):
        own[got[name]].wait()
        shared[got[name]].wait_recv()

    lane = lax.broadcasted_iota(jnp.int32, (1, 2 * LANES), 1)

    def live_mask(width):
        return (lane < width).astype(F32)

    def dot(left, right):
        return jnp.dot(left, right, preferred_element_type=F32)

    first_rhs.wait()
    first_inv.wait()
    x_first[...] = live_mask(live_width[0]) * dot(rhs_first[...].astype(BF16), w_inv_low[0, 0])
    xf[0, 0] = x_first[mine, :]
    first_out = pltpu.make_async_copy(x_first, out_f.at[0], out_local.at[0])
    first_out.start()

    pl.semaphore_wait(barrier, (ny - 1) + (nz - 1) + (NX - 1) + NX)
    first_x = remote(x_first.at[theirs], xf.at[0, 1], pair_send.at[0], pair_recv.at[0], partner)
    first_x.start()

    tab_copies = []
    for a in range(CORES):
        for dx in range(NX):
            if (a, dx) != (0, 0):
                tab_copies.append(
                    remote(
                        tabs.at[0, x],
                        tabs.at[a, x],
                        tab_send.at[len(tab_copies)],
                        tab_recv.at[len(tab_copies)],
                        at(z, c if a == 0 else other, y, lax.rem(x + dx, NX)),
                    )
                )
                tab_copies[-1].start()
    for copy in shared[:2]:
        copy.start()

    def halves(own_rows, partner_rows):
        return jnp.concatenate([own_rows, partner_rows], axis=0)

    def rows(r):
        return slice(r * PART, (r + 1) * PART)

    def chunk(ref, r, *place):
        return halves(ref[(0, *place, rows(r))], ref[(1, *place, rows(r))])

    def spread(t, r, tile):
        piece[t, r] = tile.astype(BF16)
        ring(
            lambda d: remote(
                piece.at[t, r],
                held[CHUNKS * t + r].at[y],
                spread_send.at[t, r],
                spread_recv.at[t, r],
                at(z, c, lax.rem(y + d, ny), x),
            ).start(),
            ny,
        )
        held[CHUNKS * t + r][y] = tile.astype(BF16)

    def spread_all(t, r):
        span = held[CHUNKS * t + r].at[pl.ds(0, ny - 1)]
        return remote(span, span, spread_send.at[t, r], spread_recv.at[t, r], partner)

    def choose(t, r, n, base):
        have = held[CHUNKS * t + r]
        for d in (2, 1, 3, 0):
            xx = lax.rem(x + d, NX)
            for k in range(SLOTS):
                top, low = [have[lax.div(stab[a, xx, 0, base + k], NX)].astype(F32) for a in range(CORES)]
                tile = halves(top[:PART], low[PART:]).astype(BF16)
                if d:
                    stage[t, r, n, d - 1, k] = tile
                else:
                    pick[(CHUNKS * t + r) * 2 + n][x, k] = tile
            if d:
                remote(
                    stage.at[t, r, n, d - 1],
                    pick[(CHUNKS * t + r) * 2 + n].at[x],
                    pick_send.at[t, r, n],
                    pick_recv.at[t, r, n],
                    at(z, c, y, xx),
                ).start()

    def choose_all(t, r, n):
        span = pick[(CHUNKS * t + r) * 2 + n].at[pl.ds(0, NX - 1)]
        return remote(span, span, pick_send.at[t, r, n], pick_recv.at[t, r, n], partner)

    def products(t, r, n, weights, pair, base):
        choose_all(t, r, n).wait_recv()
        for a in range(CORES):
            for k in range(SLOTS):
                column = lax.rem(stab[a, x, 0, base + k], NX)
                left = pick[(CHUNKS * t + r) * 2 + n][column, k]
                prod[a * SLOTS + k] = dot(left, weights[pair, a, k])[a * PART : (a + 1) * PART]

    def placed(base, d):
        zz = CORES * lax.rem(z + d, nz)
        totals = []
        for to, q in enumerate((zz + c, zz + other)):
            total = None
            for a in range(CORES):
                for k in range(SLOTS):
                    hit = jnp.where(stab[a, x, 0, base + k] == q, 1.0, 0.0).astype(F32)
                    term = prod[a * SLOTS + k] * hit
                    total = term if total is None else total + term
            totals.append(total)
        return halves(*totals)

    def keep(r, base):
        def one(d, carry):
            acc[r, d] = placed(base, d)
            return carry

        lax.fori_loop(0, nz, one, 0)

    def exchange(t, r, base, with_kept):
        def value(d):
            return placed(base, d) + acc[r, d] if with_kept else placed(base, d)

        def send(d):
            part[t, r, d - 1] = value(d).astype(BF16)
            remote(
                part.at[t, r, d - 1],
                landed.at[t, r, d - 1],
                sum_send.at[t, r],
                sum_recv.at[t, r],
                at(lax.rem(z + d, nz), c, y, x),
            ).start()

        ring(send, nz)
        mine_sum[r] = value(0)

    def sum_all(t, r):
        return remote(landed.at[t, r], landed.at[t, r], sum_send.at[t, r], sum_recv.at[t, r], partner)

    def summed(t, r):
        sum_all(t, r).wait_recv()
        total = mine_sum[r]
        for d in range(nz - 1):
            total = total + landed[t, r, d].astype(F32)
        return total

    in_own = lax.broadcasted_iota(jnp.int32, (ROWS, 2 * LANES), 0) < PART
    in_lane = lax.broadcasted_iota(jnp.int32, (ROWS, 2 * LANES), 1)

    def solve(level, weights, residual):
        residual = residual.astype(BF16)
        top, low = [dot(residual, weights[level, a]) for a in range(CORES)]
        width = jnp.where(in_own, stab[0, x, 0, LIVE + level], stab[1, x, 0, LIVE + level])
        return (in_lane < width).astype(F32) * halves(top[:PART], low[PART:])

    def store(ref, level, r, tile):
        for a in range(CORES):
            ref[level, a, rows(r)] = tile[a * PART : (a + 1) * PART]

    out_copies = []

    def put(out, values, level):
        n = len(out_copies) // 2
        out_copies.append(pltpu.make_async_copy(values.at[level, 0], out.at[level, mine], out_local.at[1 + n]))
        out_copies.append(remote(values.at[level, 1], out.at[level, mine], out_send.at[n], out_recv.at[n], partner))
        out_copies[-2].start()
        out_copies[-1].start()

    chunks = range(CHUNKS)

    first_x.wait_recv()
    for r in chunks:
        spread(0, r, chunk(xf.at[0], r))
    for copy in shared[2:]:
        copy.start()
    for copy in tab_copies:
        copy.wait_recv()
    to_scalar = pltpu.make_async_copy(tabs, stab, tab_local)
    to_scalar.start()
    to_scalar.wait()

    def gather(t, base, crit):
        for r in chunks:
            spread_all(t, r).wait_recv()
            choose(t, r, 0, base + SLOTS * crit)

    def multiply(t, weights, name, source, target, crit, late):
        need((name, crit))
        for r in chunks:
            products(t, r, 0, weights, crit, source + SLOTS * crit)
            exchange(t, r, target + SLOTS * crit, late is None)
            if late is not None:
                choose(t, r, 1, source + SLOTS * late)

    def multiply_late(t, r, weights, name, source, target, late):
        if r == 0:
            need((name, late))
        products(t, r, 1, weights, late, source + SLOTS * late)
        keep(r, target + SLOTS * late)

    gather(0, LOW_SOURCE, 0)
    multiply(0, w_low, "low", LOW_SOURCE, LOW_TARGET, 0, 1)
    need("rhs")
    need("inv_low")
    for r in chunks:
        solved = solve(1, w_inv_low, chunk(rhs_rest, r, 0) - summed(0, r))
        spread(1, r, solved)
        store(xf, 1, r, solved)
        multiply_late(0, r, w_low, "low", LOW_SOURCE, LOW_TARGET, 1)
    put(out_f, xf, 1)

    gather(1, LOW_SOURCE, 2)
    multiply(1, w_low, "low", LOW_SOURCE, LOW_TARGET, 2, None)
    need("inv_up")
    for r in chunks:
        solved = solve(2, w_inv_low, chunk(rhs_rest, r, 1) - summed(1, r))
        back = solve(2, w_inv_up, solved)
        spread(2, r, back)
        store(xf, 2, r, solved)
        store(yb, 2, r, back)
    put(out_f, xf, 2)
    put(out_b, yb, 2)

    gather(2, UP_SOURCE, 2)
    multiply(2, w_up, "up", UP_SOURCE, UP_TARGET, 2, 1)
    for r in chunks:
        back = solve(1, w_inv_up, chunk(xf.at[1], r) - summed(2, r))
        spread(3, r, back)
        store(yb, 1, r, back)
        multiply_late(2, r, w_up, "up", UP_SOURCE, UP_TARGET, 1)
    put(out_b, yb, 1)

    gather(3, UP_SOURCE, 0)
    multiply(3, w_up, "up", UP_SOURCE, UP_TARGET, 0, None)
    for r in chunks:
        store(yb, 0, r, solve(0, w_inv_up, chunk(xf.at[0], r) - summed(3, r)))
    put(out_b, yb, 0)

    first_out.wait()
    first_x.wait_send()
    for copy in shared + tab_copies:
        copy.wait_send()
    for t in range(4):
        for r in chunks:
            spread_all(t, r).wait_send()
            choose_all(t, r, 0).wait_send()
            if t % 2 == 0:
                choose_all(t, r, 1).wait_send()
            sum_all(t, r).wait_send()
    for copy in out_copies:
        copy.wait()


def deliver(forward, backward, out_f, out_b, sem):
    copies = [
        pltpu.make_async_copy(src.at[level], dst.at[level], sem.at[n, level])
        for n, (src, dst) in enumerate(((forward, out_f), (backward, out_b)))
        for level in range(3)
    ]
    for copy in copies:
        copy.start()
    for copy in copies:
        copy.wait()


def local(
    ny,
    nz,
    right_side,
    live_width,
    lower_inverse,
    upper_inverse,
    lower_blocks,
    lower_source,
    lower_target,
    upper_blocks,
    upper_source,
    upper_target,
):
    levels, _, _, count, width = right_side.shape
    dma = pltpu.SemaphoreType.DMA
    hbm = pl.BlockSpec(memory_space=pl.ANY)
    out = jax.ShapeDtypeStruct((levels, count, width), F32)
    forward, backward = pl.pallas_call(
        functools.partial(kernel, ny, nz),
        out_shape=(pltpu.VMEM(out.shape, F32), pltpu.VMEM(out.shape, F32)),
        in_specs=[hbm] + [pl.BlockSpec(memory_space=pltpu.SMEM)] * 5 + [hbm] * 4,
        out_specs=(hbm, hbm),
        scratch_shapes=[
            pltpu.VMEM((count, width), F32),
            pltpu.VMEM((CORES, levels - 1, CHUNKS * PART, width), F32),
            pltpu.VMEM((levels, CORES, width, width), BF16),
            pltpu.VMEM((levels, CORES, width, width), BF16),
            pltpu.VMEM((levels, CORES, SLOTS, width, width), BF16),
            pltpu.VMEM((levels, CORES, SLOTS, width, width), BF16),
            pltpu.VMEM((count, width), F32),
            pltpu.VMEM((levels, CORES, CHUNKS * PART, width), F32),
            pltpu.VMEM((levels, CORES, CHUNKS * PART, width), F32),
            pltpu.VMEM((4, CHUNKS, ROWS, width), BF16),
            [pltpu.VMEM((ny, ROWS, width), BF16) for _ in range(4 * CHUNKS)],
            pltpu.VMEM((4, CHUNKS, 2, NX - 1, SLOTS, ROWS, width), BF16),
            [pltpu.VMEM((NX, SLOTS, ROWS, width), BF16) for _ in range(8 * CHUNKS)],
            pltpu.VMEM((CORES * SLOTS, PART, width), F32),
            pltpu.VMEM((CHUNKS, nz, ROWS, width), F32),
            pltpu.VMEM((CHUNKS, ROWS, width), F32),
            pltpu.VMEM((4, CHUNKS, nz - 1, ROWS, width), BF16),
            pltpu.VMEM((4, CHUNKS, nz - 1, ROWS, width), BF16),
            pltpu.VMEM((CORES, NX, 8, LANES), jnp.int32),
            pltpu.SMEM((CORES, NX, 8, LANES), jnp.int32),
            dma((11,)),
            dma((10,)),
            dma((10,)),
            dma((7,)),
            dma((7,)),
            dma(()),
            dma((4, CHUNKS)),
            dma((4, CHUNKS)),
            dma((4, CHUNKS, 2)),
            dma((4, CHUNKS, 2)),
            dma((4, CHUNKS)),
            dma((4, CHUNKS)),
            dma((6,)),
            dma((5,)),
            dma((5,)),
        ],
        compiler_params=pltpu.CompilerParams(collective_id=0, has_side_effects=True, vmem_limit_bytes=60 << 20),
        cost_estimate=pl.CostEstimate(flops=252 << 20, bytes_accessed=8 << 20, transcendentals=0),
    )(
        right_side.reshape(levels, count, width),
        live_width.reshape(levels),
        lower_source,
        lower_target,
        upper_source,
        upper_target,
        lower_inverse.reshape(levels, width, width),
        upper_inverse.reshape(levels, width, width),
        lower_blocks.reshape(levels, SLOTS, width, width),
        upper_blocks.reshape(levels, SLOTS, width, width),
    )
    forward, backward = pl.pallas_call(
        deliver,
        out_shape=(out, out),
        in_specs=[pl.BlockSpec(memory_space=pltpu.VMEM), pl.BlockSpec(memory_space=pltpu.VMEM)],
        out_specs=(hbm, hbm),
        scratch_shapes=[dma((2, 3))],
        compiler_params=pltpu.CompilerParams(vmem_limit_bytes=1 << 20),
        cost_estimate=pl.CostEstimate(flops=0, bytes_accessed=1 << 20, transcendentals=0),
    )(forward, backward)
    return forward[:, None, None], backward[:, None, None]


def solution(mesh):
    placed = (
        P(None, "prow", "pcol", None, None),
        P(None, "prow", "pcol"),
        P(None, "prow", "pcol", None, None),
        P(None, "prow", "pcol", None, None),
        P(None, "prow", "pcol", None, None, None),
        P(None, "prow", "pcol", None),
        P(None, "prow", "pcol", None),
        P(None, "prow", "pcol", None, None, None),
        P(None, "prow", "pcol", None),
        P(None, "prow", "pcol", None),
    )
    return jax.shard_map(
        functools.partial(local, mesh.shape["pcol"] // NX, mesh.shape["prow"] // CORES),
        mesh=mesh,
        in_specs=placed,
        out_specs=(P(None, "prow", "pcol", None, None), P(None, "prow", "pcol", None, None)),
        check_vma=False,
    )
```

time: 87 us -> 83 us (0.954)
  Pallas kernels: 86.3 us -> 82.2 us
    pallas_call x1, Pallas kernels: 85.5 us -> 81.4 us  [local(): pl.pallas_call(functools.partial(kernel, ny, nz), out_shape=(pltpu.VMEM(o...]
where the time goes in v2:
time: 83 us; the launch traced here: 82.9 us
  Pallas kernels  82.2 us (99%)
    pallas_call x1, Pallas kernels, local(): pl.pallas_call(functools.partial(kernel, ny, nz), out_shape=(pltpu.VMEM(o...  81.4 us

profile of v2, /device:TPU:1, one launch (start us, length us, event | category | flops | bytes accessed | tf_op | source)
XLA Modules:
  0.0 82.9 jit_solution(4534337588760266147)
XLA Ops:
  0.6 81.4 %shard_map.113 = (f32[3,64,256]{2,1,0:T(8,128)S(1)}, f32[3,64,256]{2,1,0:T(8,128)S(1)}) custom-call(f32[3,64,256]{2,1,0:T(8,128)} %bitcast.16, s32[3]{0:T(128)} %bitcast.17, s32[3,1,1,4]{3,2,1,0:T(1,128)} %low_source.1, s32[3,1,1,4]{3,2,1,0:T(1,128)} %low_target.1, s32[3,1,1,4]{3,2,1,0:T(1,128)} %up_source.1, s32[3,1,1,4]{3,2,1,0:T(1,128)} %up_target.1, ...), custom_call_target="tpu_custom_call" | custom-call | flops 264241152 | bytes 8388608 | tf_op jit(solution)/shard_map/pallas_call | solution.py:435
  82.1 0.8 shard_map.114

commit v3 on v2

--- a/solution.py
+++ b/solution.py
@@ -200,16 +200,14 @@
 
     def spread(t, r, tile):
         piece[t, r] = tile.astype(BF16)
-        ring(
-            lambda d: remote(
+        for i in range(ny - 1):
+            remote(
                 piece.at[t, r],
                 held[CHUNKS * t + r].at[y],
                 spread_send.at[t, r],
                 spread_recv.at[t, r],
-                at(z, c, lax.rem(y + d, ny), x),
-            ).start(),
-            ny,
-        )
+                at(z, c, lax.rem(y + far(i, ny), ny), x),
+            ).start()
         held[CHUNKS * t + r][y] = tile.astype(BF16)
 
     def spread_all(t, r):
@@ -310,12 +308,15 @@
 
     out_copies = []
 
-    def put(out, values, level):
+    def put(where, own_rows, partner_rows):
         n = len(out_copies) // 2
-        out_copies.append(pltpu.make_async_copy(values.at[level, 0], out.at[level, mine], out_local.at[1 + n]))
-        out_copies.append(remote(values.at[level, 1], out.at[level, mine], out_send.at[n], out_recv.at[n], partner))
+        out_copies.append(pltpu.make_async_copy(own_rows, where, out_local.at[1 + n]))
+        out_copies.append(remote(partner_rows, where, out_send.at[n], out_recv.at[n], partner))
         out_copies[-2].start()
         out_copies[-1].start()
+
+    def put_level(out, values, level):
+        put(out.at[level, mine], values.at[level, 0], values.at[level, 1])
 
     chunks = range(CHUNKS)
 
@@ -358,7 +359,7 @@
         spread(1, r, solved)
         store(xf, 1, r, solved)
         multiply_late(0, r, w_low, "low", LOW_SOURCE, LOW_TARGET, 1)
-    put(out_f, xf, 1)
+    put_level(out_f, xf, 1)
 
     gather(1, LOW_SOURCE, 2)
     multiply(1, w_low, "low", LOW_SOURCE, LOW_TARGET, 2, None)
@@ -369,8 +370,8 @@
         spread(2, r, back)
         store(xf, 2, r, solved)
         store(yb, 2, r, back)
-    put(out_f, xf, 2)
-    put(out_b, yb, 2)
+    put_level(out_f, xf, 2)
+    put_level(out_b, yb, 2)
 
     gather(2, UP_SOURCE, 2)
     multiply(2, w_up, "up", UP_SOURCE, UP_TARGET, 2, 1)
@@ -379,13 +380,14 @@
         spread(3, r, back)
         store(yb, 1, r, back)
         multiply_late(2, r, w_up, "up", UP_SOURCE, UP_TARGET, 1)
-    put(out_b, yb, 1)
+    put_level(out_b, yb, 1)
 
     gather(3, UP_SOURCE, 0)
     multiply(3, w_up, "up", UP_SOURCE, UP_TARGET, 0, None)
     for r in chunks:
         store(yb, 0, r, solve(0, w_inv_up, chunk(xf.at[0], r) - summed(3, r)))
-    put(out_b, yb, 0)
+        there = pl.ds(pl.multiple_of(c * CHUNKS * PART + r * PART, PART), PART)
+        put(out_b.at[0, there], yb.at[0, 0, pl.ds(r * PART, PART)], yb.at[0, 1, pl.ds(r * PART, PART)])
 
     first_out.wait()
     first_x.wait_send()
@@ -470,9 +472,9 @@
             dma((4, CHUNKS, 2)),
             dma((4, CHUNKS)),
             dma((4, CHUNKS)),
-            dma((6,)),
-            dma((5,)),
-            dma((5,)),
+            dma((5 + CHUNKS,)),
+            dma((4 + CHUNKS,)),
+            dma((4 + CHUNKS,)),
         ],
         compiler_params=pltpu.CompilerParams(collective_id=0, has_side_effects=True, vmem_limit_bytes=60 << 20),
         cost_estimate=pl.CostEstimate(flops=252 << 20, bytes_accessed=8 << 20, transcendentals=0),

time: 83 us -> 83.1 us (level)
  no operation moved by 1% of the time
where the time goes in v3:
time: 83.1 us; the launch traced here: 82.9 us
  Pallas kernels  82.3 us (99%)
    pallas_call x1, Pallas kernels, local(): pl.pallas_call(functools.partial(kernel, ny, nz), out_shape=(pltpu.VMEM(o...  81.5 us

profile of v3, /device:TPU:1, one launch (start us, length us, event | category | flops | bytes accessed | tf_op | source)
XLA Modules:
  0.0 82.9 jit_solution(6601669129370243289)
XLA Ops:
  0.6 81.5 %shard_map.113 = (f32[3,64,256]{2,1,0:T(8,128)S(1)}, f32[3,64,256]{2,1,0:T(8,128)S(1)}) custom-call(f32[3,64,256]{2,1,0:T(8,128)} %bitcast.16, s32[3]{0:T(128)} %bitcast.17, s32[3,1,1,4]{3,2,1,0:T(1,128)} %low_source.1, s32[3,1,1,4]{3,2,1,0:T(1,128)} %low_target.1, s32[3,1,1,4]{3,2,1,0:T(1,128)} %up_source.1, s32[3,1,1,4]{3,2,1,0:T(1,128)} %up_target.1, ...), custom_call_target="tpu_custom_call" | custom-call | flops 264241152 | bytes 8388608 | tf_op jit(solution)/shard_map/pallas_call | solution.py:437
  82.1 0.8 shard_map.114
